TPU v7x, 256 devices: a whole 4x4x8 slice. The times are simulated.
256 devices in a mesh: ctx: 16 (over x_lo, y, core), head: 16 (over x_hi, z).
Axes of the slice: x: 4 (x_hi: 2, x_lo: 2; x = x_hi * 2 + x_lo), y: 4, z: 8, core: 2. Of those that a mesh axis runs over, the one named last changes fastest.
Arguments:
- residual: bfloat16 [4096, 4096], P('ctx', 'head'), may hold values from -84 to 84
- hyena_gain: float32 [4096], replicated, may hold values from 0.1 to 1.9
- in_weight: bfloat16 [4096, 3, 4096], P(None, None, 'head'), may hold values from -0.09375 to 0.09375
- short_filter: float32 [3, 3, 4096], P(None, None, 'head'), may hold values from -1 to 1
- decay_rate: float32 [4096, 16], P('head'), may hold values from 4.8828125e-05 to 0.033
- residue: float32 [4096, 16], P('head'), may hold values from -3 to 3
- skip_gain: float32 [4096], P('head'), may hold values from -1 to 1
- attn_gain: float32 [4096], replicated, may hold values from 0.1 to 1.9
- qkv_weight: bfloat16 [4096, 3, 2048], P(None, None, 'head'), may hold values from -0.1328125 to 0.1328125
Outputs:
- mixed: bfloat16 [4096, 4096], P('ctx', 'head')
- attended: bfloat16 [4096, 2048], P('ctx', 'head')
All inputs are finite; a program needn't handle non-finite values.
Results may differ from a plain program's by a relative error of at most 0.02.
The roundings to bfloat16 on the way count: a program that leaves them out, or rounds other values in their place, can miss the bound.
Values may be sent and summed in bfloat16 or wider, within the bound.
A program may use at most 128 MiB of HBM per device.

v0:
```python
import jax
import jax.numpy as jnp
from jax import lax
from jax.sharding import PartitionSpec as P

HD = 128


eps = 1e-06
rotary_base = 10000.0
highest = lax.Precision.HIGHEST


def combine_states(first_pair, second_pair):
    return (first_pair[0] * second_pair[0], second_pair[0] * first_pair[1] + second_pair[1])


def block_parts(product, decays, modal):
    span_len = 128
    lag_steps = jnp.arange(span_len).astype(jnp.float32)
    filt_lags = jnp.einsum(
        "cn,cnd->cd", modal, jnp.exp(-decays[:, :, None] * lag_steps), precision=highest
    )
    offsets = jnp.arange(span_len)[:, None] - jnp.arange(span_len)[None, :]
    toeplitz = jnp.where(offsets[None] >= 0, filt_lags[:, jnp.maximum(offsets, 0)], 0.0)
    block_count = product.shape[0] // span_len
    pieces = product.reshape(block_count, span_len, product.shape[1])
    intra = jnp.einsum("cts,bsc->btc", toeplitz, pieces, precision=highest).reshape(product.shape)
    tail_pows = jnp.exp(-decays[:, :, None] * (span_len - 1.0 - lag_steps))
    ends = jnp.einsum("bsc,cns->bcn", pieces, tail_pows, precision=highest)
    return (intra, ends, span_len)


def chain(ends, decays, span_len, state_zero):
    block_count = ends.shape[0]
    step_decay = jnp.broadcast_to(jnp.exp(-decays * span_len), ends.shape)
    inclusive = lax.associative_scan(combine_states, (step_decay, ends))[1]
    order = jnp.arange(block_count).astype(jnp.float32)
    powers = jnp.exp(-decays[None] * (span_len * order)[:, None, None])
    starts = (
        jnp.concatenate([jnp.zeros_like(ends[:1]), inclusive[:-1]], axis=0)
        + powers * state_zero[None]
    )
    final_state = inclusive[-1] + jnp.exp(-decays * (span_len * block_count)) * state_zero
    return (starts, final_state)


def spread(starts, decays, modal, span_len):
    lag_steps = jnp.arange(span_len).astype(jnp.float32)
    rise_table = modal[:, :, None] * jnp.exp(-decays[:, :, None] * (lag_steps + 1.0))
    return jnp.einsum("bcn,cnt->btc", starts, rise_table, precision=highest).reshape(
        -1, starts.shape[1]
    )


def long_conv(product, decays, modal):
    intra, ends, span_len = block_parts(product, decays, modal)
    starts = chain(ends, decays, span_len, jnp.zeros(decays.shape, jnp.float32))[0]
    return intra + spread(starts, decays, modal, span_len)


def filter_coef(decay_rate, residue):
    return residue * jnp.sqrt(-jnp.expm1(-2.0 * decay_rate))


def short_conv(padded, taps):
    return taps[0] * padded[2:] + taps[1] * padded[1:-1] + taps[2] * padded[:-2]


def hyena_mix(streams, decays, modal, skip):
    product = streams[:, 1] * streams[:, 2]
    return streams[:, 0] * (long_conv(product, decays, modal) + skip * product)


def rotate(values, positions):
    half_dim = values.shape[-1] // 2
    inverse = jnp.exp(-jnp.log(rotary_base) * jnp.arange(half_dim).astype(jnp.float32) / half_dim)
    angle = positions[:, None] * inverse[None, :]
    cosine = jnp.cos(angle)[:, None, :]
    sine = jnp.sin(angle)[:, None, :]
    first_half = values[..., :half_dim]
    second_half = values[..., half_dim:]
    return jnp.concatenate(
        [first_half * cosine - second_half * sine, second_half * cosine + first_half * sine],
        axis=-1,
    )


def local(
    residual,
    hyena_gain,
    in_weight,
    short_filter,
    decay_rate,
    residue,
    skip_gain,
    attn_gain,
    qkv_weight,
):
    tok_rows = residual.shape[0]
    local_width = residual.shape[1]
    full_width = hyena_gain.shape[0]

    def make_fold(gain, weight):
        flat_weight = weight.reshape(weight.shape[0], -1)

        def add_piece(carry, piece, start):
            piece_f = piece.astype(jnp.float32)
            scaled = (piece_f * gain).astype(jnp.bfloat16)
            summed = jnp.dot(scaled, flat_weight, preferred_element_type=jnp.float32)
            return (summed, jnp.sum(piece_f * piece_f, axis=1))

        start_carry = (
            jnp.zeros((tok_rows, flat_weight.shape[1]), jnp.float32),
            jnp.zeros((tok_rows,), jnp.float32),
        )
        return (add_piece, start_carry)

    def finish(carry):
        summed, squares = carry
        return summed * lax.rsqrt(squares / full_width + eps)[:, None]

    fold_hyena, carry_hyena = make_fold(hyena_gain, in_weight)
    hyena_proj = finish(
        fold_hyena(carry_hyena, lax.all_gather(residual, "head", axis=1, tiled=True), jnp.int32(0))
    )
    streams_bf = hyena_proj.astype(jnp.bfloat16).reshape(tok_rows, 3, local_width)
    modal = filter_coef(decay_rate, residue)
    share = local_width // lax.axis_size("ctx")
    offset = lax.axis_index("ctx") * share
    channels = lax.all_to_all(streams_bf, "ctx", split_axis=2, concat_axis=0, tiled=True)
    padded = jnp.pad(channels.astype(jnp.float32), ((2, 0), (0, 0), (0, 0)))
    taps = lax.dynamic_slice_in_dim(short_filter, offset, share, 2)
    decay_part = lax.dynamic_slice_in_dim(decay_rate, offset, share, 0)
    modal_part = lax.dynamic_slice_in_dim(modal, offset, share, 0)
    skip_part = lax.dynamic_slice_in_dim(skip_gain, offset, share, 0)
    gated_part = hyena_mix(short_conv(padded, taps), decay_part, modal_part, skip_part)
    gated = lax.all_to_all(gated_part, "ctx", split_axis=0, concat_axis=1, tiled=True)
    mixed = (residual.astype(jnp.float32) + gated).astype(jnp.bfloat16)
    fold_attn, carry_attn = make_fold(attn_gain, qkv_weight)
    local_heads = qkv_weight.shape[2] // HD
    projected = finish(
        fold_attn(carry_attn, lax.all_gather(mixed, "head", axis=1, tiled=True), jnp.int32(0))
    )
    projected = projected.reshape(tok_rows, 3, local_heads, HD)
    first_row = lax.axis_index("ctx") * tok_rows
    query_pos = first_row + jnp.arange(tok_rows)
    positions = query_pos.astype(jnp.float32)
    queries = rotate(projected[:, 0], positions).astype(jnp.bfloat16)
    keys = rotate(projected[:, 1], positions).astype(jnp.bfloat16).reshape(tok_rows, -1)
    values = projected[:, 2].astype(jnp.bfloat16).reshape(tok_rows, -1)
    last_row = first_row + tok_rows - 1
    factor = 1.0 / HD**0.5
    start_state = (
        jnp.full((local_heads, tok_rows), -1e30, jnp.float32),
        jnp.zeros((local_heads, tok_rows), jnp.float32),
        jnp.zeros((local_heads, tok_rows, HD), jnp.float32),
    )
    key_piece = lax.all_gather(keys, "ctx", axis=0, tiled=True)
    value_piece = lax.all_gather(values, "ctx", axis=0, tiled=True)
    length = key_piece.shape[0]
    sub_len = 1024

    def one_sub(step_index, state):
        best, totals, summed = state
        begin = step_index * sub_len
        key_sub = lax.dynamic_slice_in_dim(key_piece, begin, sub_len, 0).reshape(
            sub_len, local_heads, HD
        )
        value_sub = lax.dynamic_slice_in_dim(value_piece, begin, sub_len, 0).reshape(
            sub_len, local_heads, HD
        )
        scores = (
            jnp.einsum("qhd,khd->hqk", queries, key_sub, preferred_element_type=jnp.float32)
            * factor
        )
        key_pos = begin + jnp.arange(sub_len)
        scores = jnp.where(key_pos[None, None, :] <= query_pos[None, :, None], scores, -1e30)
        new_best = jnp.maximum(best, jnp.max(scores, axis=2))
        rescale = jnp.exp(best - new_best)
        weights = jnp.exp(scores - new_best[:, :, None])
        totals = totals * rescale + jnp.sum(weights, axis=2)
        update = jnp.einsum(
            "hqk,khd->hqd",
            weights.astype(jnp.bfloat16),
            value_sub,
            preferred_element_type=jnp.float32,
        )
        return (new_best, totals, summed * rescale[:, :, None] + update)

    def compute(state):
        return lax.fori_loop(0, length // sub_len, one_sub, state)

    def unchanged(state):
        return state

    best, totals, summed = lax.cond(jnp.int32(0) <= last_row, compute, unchanged, start_state)
    attended = (
        (summed / totals[:, :, None]).transpose(1, 0, 2).reshape(tok_rows, -1).astype(jnp.bfloat16)
    )
    return (mixed, attended)


def solution(mesh):
    return jax.shard_map(
        local,
        mesh=mesh,
        in_specs=(
            P("ctx", "head"),
            P(),
            P(None, None, "head"),
            P(None, None, "head"),
            P("head", None),
            P("head", None),
            P("head"),
            P(),
            P(None, None, "head"),
        ),
        out_specs=(P("ctx", "head"), P("ctx", "head")),
        check_vma=False,
    )
```

profile of v0, /device:TPU:3, one launch (start us, length us, event | category | flops | bytes accessed | tf_op | source)
XLA Modules:
  0.0 409.4 jit_solution(10289013227650564379)
XLA Ops:
  7.9 8.7 %copy.83 = bf16[4096,3,256]{0,2,1:T(8,128)(2,1)} copy(bf16[4096,3,256]{2,0,1:T(8,128)(2,1)} %param.15) | data formatting | bytes 12582912 | tf_op args[2]
  17.1 77.3 %all-gather.6.cloned.1.call-done = bf16[256,4096]{1,0:T(8,128)(2,1)} async-done(((bf16[256,256]{1,0:T(8,128)(2,1)}), bf16[256,4096]{1,0:T(8,128)(2,1)}) %all-gather.6.cloned.1.call-update) | async-done | bytes 2097168 | tf_op jit(solution)/shard_map/all_gather | solution.py:125
  94.4 2.1 fusion.16
  96.5 5.3 %fusion.28 = bf16[256,768]{1,0:T(8,128)(2,1)S(1)} fusion(bf16[4096,768]{0,1:T(8,128)(2,1)} %bitcast.114, bf16[256,4096]{1,0:T(8,128)(2,1)} %all-gather.6.cloned.1.call-done, f32[4096]{0:T(1024)S(1)} %copy-done.5, f32[256]{0:T(256)S(1)} %add_rsqrt_fusion.1), kind=kOutput, calls=%fused_computation.37 | convolution fusion | flops 1614151680 | bytes 8799232 | tf_op jit(solution)/shard_map/dot_general | solution.py:110
  103.2 9.1 %all-to-all-start = ((bf16[256,3,256]{0,1,2:T(4,128)(2,1)}), bf16[256,3,256]{0,1,2:T(4,128)(2,1)S(1)}, u32[]{:S(2)}, u32[]{:S(2)}) async-start(bf16[256,3,256]{0,1,2:T(4,128)(2,1)} %copy.85), calls=%async_computation | async-start | bytes 1048576 | tf_op jit(solution)/shard_map/all_to_all | solution.py:131
  112.9 54.5 %gather_fusion = f32[16384,16]{1,0:T(8,128)} fusion(f32[16,128]{0,1:T(8,128)S(1)} %copy.104, s32[16384]{0:T(1024)S(1)} %bitcast_clamp_fusion), kind=kCustom, calls=%fused_computation | custom fusion | bytes 2162688 | tf_op jit(solution)/shard_map/gather | solution.py:25
  167.4 5.2 %copy.89 = f32[128,128,16]{1,0,2:T(8,128)S(1)} copy(f32[128,128,16]{2,1,0:T(8,128)} %bitcast.113) | data formatting | bytes 2097152 | tf_op jit(solution)/shard_map/gather | solution.py:25
  192.1 6.4 %pad.80 = f32[32,16,16]{0,2,1:T(8,128)} pad(f32[16,16,16]{0,2,1:T(8,128)S(1)} %add.218, f32[]{:T(128)} %constant.97.clone.1), padding=1_0_1x0_0_0x0_0_0 | pad | bytes 49156
  198.5 1.7 convolution_bitcast_fusion.2
  201.3 2.2 fusion.34
  208.2 5.7 %all-to-all-start.1 = ((f32[16,256,16]{1,2,0:T(8,128)}), f32[16,256,16]{1,2,0:T(8,128)S(1)}, u32[]{:S(2)}, u32[]{:S(2)}) async-start(f32[16,256,16]{1,2,0:T(8,128)} %copy.93), calls=%async_computation.1 | async-start | bytes 524288 | tf_op jit(solution)/shard_map/all_to_all | solution.py:138
  214.9 5.5 %all-to-all-done.1 = f32[16,256,16]{1,2,0:T(8,128)S(1)} async-done(((f32[16,256,16]{1,2,0:T(8,128)}), f32[16,256,16]{1,2,0:T(8,128)S(1)}, u32[]{:S(2)}, u32[]{:S(2)}) %all-to-all-start.1) | async-done | bytes 262176 | tf_op jit(solution)/shard_map/all_to_all | solution.py:138
  221.4 2.9 copy.94
  224.3 74.3 %all-gather.8.cloned.1.call-done = bf16[256,4096]{0,1:T(8,128)(2,1)} async-done(((bf16[256,256]{0,1:T(8,128)(2,1)}), bf16[256,4096]{0,1:T(8,128)(2,1)}) %all-gather.8.cloned.1.call-update) | async-done | bytes 2097168 | tf_op jit(solution)/shard_map/all_gather | solution.py:143
  298.6 2.2 fusion.18
  300.8 4.4 %fusion.31 = f32[256,384]{1,0:T(8,128)S(1)} fusion(bf16[4096,384]{0,1:T(8,128)(2,1)} %bitcast.118, bf16[256,4096]{0,1:T(8,128)(2,1)} %all-gather.8.cloned.1.call-done, f32[4096]{0:T(1024)S(1)} %copy-done.6, f32[256]{0:T(256)S(1)} %add_rsqrt_fusion), kind=kOutput, calls=%fused_computation.38 | convolution fusion | flops 808550400 | bytes 5653504 | tf_op jit(solution)/shard_map/dot_general | solution.py:110
  307.9 36.3 %all-gather.10.cloned.1.call-done = bf16[4096,128]{0,1:T(8,128)(2,1)} async-done(((bf16[256,128]{0,1:T(8,128)(2,1)}), bf16[4096,128]{0,1:T(8,128)(2,1)}) %all-gather.10.cloned.1.call-update) | async-done | bytes 1048592 | tf_op jit(solution)/shard_map/all_gather | solution.py:159
  344.2 38.3 %all-gather.12.cloned.1.call-done = bf16[4096,1,1,128]{0,3,1,2:T(8,128)(2,1)} async-done(((bf16[256,1,1,128]{0,3,1,2:T(8,128)(2,1)}), bf16[4096,1,1,128]{0,3,1,2:T(8,128)(2,1)}) %all-gather.12.cloned.1.call-update) | async-done | bytes 1048592 | tf_op jit(solution)/shard_map/all_gather | solution.py:160
  382.5 18.7 %conditional.1 = (f32[1,256]{1,0:T(1,128)}, f32[1,256,128]{2,1,0:T(8,128)}) conditional(s32[]{:T(128)} %convert_element_type.123, () %tuple.30, (s32[]{:T(128)}, s32[256]{0:T(256)S(1)}, bf16[4096,128]{0,1:T(8,128)(2,1)}, bf16[256,1,128]{0,2,1:T(8,128)(2,1)S(1)}, bf16[4096,128]{0,1:T(8,128)(2,1)}) %tuple.88), branch_computations={%region_2.3_spmd, %region_3.8_spmd} | conditional | flops 136415744 | bytes 4156735 | solution.py:197
  382.6 18.6 %while.17 = (s32[]{:T(128)}, f32[1,256]{1,0:T(1,128)S(1)}, f32[1,256]{1,0:T(1,128)}, f32[1,256,128]{2,1,0:T(8,128)}, s32[256]{0:T(256)S(1)}, /*index=5*/bf16[409...) while((s32[]{:T(128)}, f32[1,256]{1,0:T(1,128)S(1)}, ...), condition=%wide.region_7.7_spmd.clone, body=%wide.region_4.6_spmd.clone.sunk | while | flops 136415488 | bytes 4023491 | solution.py:192
  384.8 2.0 fusion.106
  389.6 2.0 fusion.106
  394.4 2.0 fusion.106
  399.2 2.0 fusion.106
  (136 shorter events, 45.1 us)
Async XLA Ops:
  7.2 87.3 %all-gather.6.cloned.1.call-start = ((), (), s32[]{:S(2)}) async-start(), calls=%async_computation.2 | async-start | bytes 2228224 | tf_op jit(solution)/shard_map/all_gather | solution.py:125
  7.9 8.8 %copy-start.2 = (f32[256,16]{0,1:T(8,128)S(1)}, f32[256,16]{0,1:T(8,128)}, u32[]{:S(2)}) copy-start(f32[256,16]{0,1:T(8,128)} %param.17) | copy-start | bytes 49156
  7.9 8.8 %copy-start.3 = (f32[256,16]{0,1:T(8,128)S(1)}, f32[256,16]{0,1:T(8,128)}, u32[]{:S(2)}) copy-start(f32[256,16]{0,1:T(8,128)} %param.18) | copy-start | bytes 49156
  7.9 88.6 %copy-start.5 = (f32[4096]{0:T(1024)S(1)}, f32[4096]{0:T(1024)}, u32[]{:S(2)}) copy-start(f32[4096]{0:T(1024)} %param.14) | copy-start | bytes 49156
  103.2 71.1 %all-to-all-start = ((bf16[256,3,256]{0,1,2:T(4,128)(2,1)}), bf16[256,3,256]{0,1,2:T(4,128)(2,1)S(1)}, u32[]{:S(2)}, u32[]{:S(2)}) async-start(bf16[256,3,256]{0,1,2:T(4,128)(2,1)} %copy.85), calls=%async_computation | async-start | bytes 1048576 | tf_op jit(solution)/shard_map/all_to_all | solution.py:131
  167.4 5.6 %copy-start.7 = (f32[256]{0:T(256)S(1)}, f32[256]{0:T(256)}, u32[]{:S(2)}) copy-start(f32[256]{0:T(256)} %param.19) | copy-start | bytes 3076
  167.4 6.8 %copy-start.4 = (f32[3,3,256]{2,1,0:T(4,128)S(1)}, f32[3,3,256]{2,1,0:T(4,128)}, u32[]{:S(2)}) copy-start(f32[3,3,256]{2,1,0:T(4,128)} %param.16) | copy-start | bytes 27652
  200.2 21.2 %copy-start = (bf16[4096,3,128]{2,0,1:T(8,128)(2,1)S(1)}, bf16[4096,3,128]{2,0,1:T(8,128)(2,1)}, u32[]{:S(2)}) copy-start(bf16[4096,3,128]{2,0,1:T(8,128)(2,1)} %param.21) | copy-start | bytes 9437188
  208.2 12.3 %all-to-all-start.1 = ((f32[16,256,16]{1,2,0:T(8,128)}), f32[16,256,16]{1,2,0:T(8,128)S(1)}, u32[]{:S(2)}, u32[]{:S(2)}) async-start(f32[16,256,16]{1,2,0:T(8,128)} %copy.93), calls=%async_computation.1 | async-start | bytes 524288 | tf_op jit(solution)/shard_map/all_to_all | solution.py:138
  213.9 84.7 %all-gather.8.cloned.1.call-start = ((), (), s32[]{:S(2)}) async-start(), calls=%async_computation.3 | async-start | bytes 2228224 | tf_op jit(solution)/shard_map/all_gather | solution.py:143
  221.2 123.0 %all-gather.10.cloned.1.call-start = ((), (), s32[]{:S(2)}) async-start(), calls=%async_computation.4 | async-start | bytes 1114112 | tf_op jit(solution)/shard_map/all_gather | solution.py:159
  221.4 79.3 %copy-start.6 = (f32[4096]{0:T(1024)S(1)}, f32[4096]{0:T(1024)}, u32[]{:S(2)}) copy-start(f32[4096]{0:T(1024)} %param.20) | copy-start | bytes 49156
  300.8 6.4 %copy-start.1 = (bf16[256,256]{0,1:T(8,128)(2,1)S(1)}, bf16[256,256]{0,1:T(8,128)(2,1)}, u32[]{:S(2)}) copy-start(bf16[256,256]{0,1:T(8,128)(2,1)} %fusion.41) | copy-start | bytes 393220
  306.4 76.0 %all-gather.12.cloned.1.call-start = ((), (), s32[]{:S(2)}) async-start(), calls=%async_computation.5 | async-start | bytes 1114112 | tf_op jit(solution)/shard_map/all_gather | solution.py:160
Sparse Core Ops, SparseCore 0:
  10.5 83.9 all-gather.5
  221.3 77.2 all-gather.7
  306.6 37.5 all-gather.9
  345.8 36.6 all-gather.11
where the time goes:
time: 412 us; the launch traced here: 409 us
  waiting for transfers between devices  232 us (56%)
  local copies, waits for them, and re-layouts  101 us (25%)
  matrix products  27.4 us (7%)
  other arithmetic  19.2 us (5%)
  starting transfers between devices  15.2 us (4%)
  between operations  14.2 us (3%)
    all_gather x1, waiting for transfers between devices, local(): lax.all_gather(residual, 'head', axis=1, tiled=True)  77.3 us
    all_gather x1, waiting for transfers between devices, local(): lax.all_gather(mixed, 'head', axis=1, tiled=True)  74.3 us
    gather x2, local copies, waits for them, and re-layouts, block_parts(): filt_lags[:, jnp.maximum(offsets, 0)]  59.7 us
    all_gather x1, waiting for transfers between devices, local(): value_piece = lax.all_gather(values, 'ctx', axis=0, tiled=True)  38.3 us
    all_gather x1, waiting for transfers between devices, local(): key_piece = lax.all_gather(keys, 'ctx', axis=0, tiled=True)  36.3 us
    unnamed x26, local copies, waits for them, and re-layouts  21.1 us
    dot_general x2, matrix products, add_piece(): summed = jnp.dot(scaled, flat_weight, preferred_element_type=jnp.float32)  9.7 us
    all_to_all x1, starting transfers between devices, local(): lax.all_to_all(streams_bf, 'ctx', split_axis=2, concat_axis=0, tiled=True)  9.11 us
  transfers between devices with their start and end apart: 6, of which 5 were waited for; matrix products, arithmetic and copies ran while one was open for 19% of the time, Pallas kernels for 0%

commit v1 on v0

v1 whole, which is shorter than its diff:
```python
import functools

import jax
import jax.numpy as jnp
import numpy as np
from jax import lax
from jax.experimental import pallas as pl
from jax.experimental.pallas import tpu as pltpu
from jax.sharding import PartitionSpec as P

MESH = pl.DeviceIdType.MESH
f32 = jnp.float32
bf16 = jnp.bfloat16

HD = 128
EPS = 1e-6
ROWS = 256
WIDTH = 256
NH = 16
NC = 16
NZ = 8
MODES = 16
SPAN = 32
CHUNKS = 8
XFIRST = 112


def rope_tables():
    half = HD // 2
    inverse = 10000.0 ** (-np.arange(half) / half)

    def table(positions):
        angle = positions[:, None] * inverse[None, :]
        cos, sin = np.cos(angle), np.sin(angle)
        return np.concatenate([cos, cos, sin, sin], axis=1).astype(np.float32)

    return table(np.arange(NC) * float(ROWS)), table(np.arange(ROWS) * 1.0)


def kernel(
    res, hgain, w1, taps, decay, residue, skip, again, w2, far, near,
    mixed, attended,
    g1, g2, w1s, w2s, acc1, acc2, sq, strm, halo_out, halo_in,
    mode_a, mode_p, mode_f, modal, upad, qs, conv, ends, gate, e_out, e_in,
    cs, qrot, kv, kvs, m_s, l_s, o_s,
    wsem, gs, gr, hsem, es, er, ks, kr, fs,
):
    c = lax.axis_index("ctx")
    h = lax.axis_index("head")
    core = lax.rem(c, 2)
    sgn = 1 - 2 * core
    z = lax.rem(h, NZ)
    xh = h // NZ
    chip = c // 2

    def head(x, zz):
        return x * NZ + lax.rem(zz + 2 * NZ, NZ)

    partner = head(1 - xh, z)
    ahead = head(xh, z + sgn)
    behind = head(xh, z - sgn)

    wcopies = []
    for j in range(3):
        wcopies.append(pltpu.make_async_copy(w1.at[j], w1s.at[:, pl.ds(j * WIDTH, WIDTH)], wsem.at[j]))
    for j in range(3):
        wcopies.append(pltpu.make_async_copy(w2.at[j], w2s.at[:, pl.ds(j * HD, HD)], wsem.at[3 + j]))
    for copy in wcopies:
        copy.start()

    barrier = pltpu.get_barrier_semaphore()
    for to in (partner, ahead, behind):
        pl.semaphore_signal(barrier, inc=1, device_id={"head": to}, device_id_type=MESH)
    for k in range(1, NC):
        pl.semaphore_signal(
            barrier, inc=1, device_id={"ctx": lax.rem(c + k, NC)}, device_id_type=MESH
        )
    pl.semaphore_wait(barrier, NC + 2)

    sends = []
    parts = ((ROWS - XFIRST, XFIRST), (0, ROWS - XFIRST))

    def gather(own, g, which, prepare, fold):
        count = [0]

        def copy(part, org, to, index, src=None):
            lo, n = parts[part]
            dst = g.at[org, pl.ds(lo, n)]
            return pltpu.make_async_remote_copy(
                src_ref=dst if src is None else src.at[pl.ds(lo, n)],
                dst_ref=dst,
                send_sem=gs.at[which, index],
                recv_sem=gr.at[which, part, org],
                device_id={"head": to},
                device_id_type=MESH,
            )

        def send(part, org, to, src=None):
            one = copy(part, org, to, count[0], src)
            count[0] += 1
            one.start()
            sends.append(one)

        def wait(part, org):
            copy(part, org, partner, 0).wait_recv()

        send(0, h, partner, own)
        send(0, h, ahead, own)
        send(0, h, behind, own)
        send(1, h, ahead, own)
        send(1, h, behind, own)
        send(1, h, partner, own)
        prepare()
        fold(h, own, True)
        wait(0, partner)
        send(0, partner, behind)
        send(0, partner, ahead)
        late = [partner]
        for d in range(1, 5):
            a, b = head(xh, z - sgn * d), head(xh, z + sgn * d)
            a2, b2 = head(1 - xh, z - sgn * d), head(1 - xh, z + sgn * d)
            wait(0, a)
            if d < 4:
                send(0, a, ahead)
                wait(0, b)
            if d < 3:
                send(0, b, behind)
            wait(1, a)
            if d < 4:
                send(1, a, ahead)
            send(1, a, partner)
            if d < 4:
                wait(1, b)
                if d < 3:
                    send(1, b, behind)
                send(1, b, partner)
            wait(0, b2)
            if d < 4:
                send(0, b2, behind)
                wait(0, a2)
            if d < 3:
                send(0, a2, ahead)
            fold(a, g.at[a], False)
            if d < 4:
                fold(b, g.at[b], False)
            for org in late:
                wait(1, org)
                fold(org, g.at[org], False)
            late = [b2] if d == 4 else [a2, b2]
        for org in late:
            wait(1, org)
            fold(org, g.at[org], False)

    def folder(gain, w, acc):
        def fold(org, ref, first):
            columns = pl.ds(pl.multiple_of(org * WIDTH, WIDTH), WIDTH)
            rows = ref[...].astype(f32)
            squares = rows * rows
            squares = squares[:, :128] + squares[:, 128:]
            scaled = (rows * gain[:, columns]).astype(bf16)
            product = jnp.dot(scaled, w[columns, :], preferred_element_type=f32)
            if first:
                sq[...] = squares
                acc[...] = product
            else:
                sq[...] += squares
                acc[...] += product

        return fold

    def row_scale(lo, n):
        total = jnp.sum(sq[pl.ds(lo, n), :], axis=1, keepdims=True)
        return lax.rsqrt(total * (1.0 / (NH * WIDTH)) + EPS)

    def tables():
        d = decay[...]
        a = jnp.exp(-d)
        mode_a[...] = a
        twice = 2.0 * d
        series = twice * (1.0 - twice * (0.5 - twice * (1.0 / 6 - twice * (1.0 / 24 - twice * (1.0 / 120)))))
        coef = residue[...] * jnp.sqrt(jnp.where(twice < 0.1, series, 1.0 - jnp.exp(-twice)))
        modal[...] = coef
        steps = lax.broadcasted_iota(jnp.int32, (CHUNKS, WIDTH), 0).astype(f32)
        for n in range(MODES):
            mode_p[n] = jnp.exp(-decay[pl.ds(n, 1), :] * (steps * SPAN))
        lags = lax.broadcasted_iota(jnp.int32, (SPAN, WIDTH), 0).astype(f32)
        filt = jnp.zeros((SPAN, WIDTH), f32)
        for n in range(MODES):
            filt = filt + modal[pl.ds(n, 1), :] * jnp.exp(-decay[pl.ds(n, 1), :] * lags)
        filt = filt + jnp.where(lags == 0.0, skip[...], 0.0)
        for t in range(SPAN):
            mode_f[t] = jnp.broadcast_to(filt[t : t + 1, :], (CHUNKS, WIDTH))
        upad[pl.ds(0, SPAN)] = jnp.zeros((SPAN, CHUNKS, WIDTH), f32)
        there = far[c]
        fc, fsn = there[:, :HD], there[:, HD:]
        nc, ns = near[:, pl.ds(0, HD)], near[:, pl.ds(HD, HD)]
        cs[:, pl.ds(0, HD)] = nc * fc - ns * fsn
        lane = lax.broadcasted_iota(jnp.int32, (ROWS, HD), 1)
        sine = ns * fc + nc * fsn
        cs[:, pl.ds(HD, HD)] = jnp.where(lane < HD // 2, -sine, sine)

    def before_first():
        tables()
        for copy in wcopies[:3]:
            copy.wait()

    gather(res, g1, 0, before_first, folder(hgain, w1s, acc1))

    for k in range(6):
        strm[k, pl.ds(0, 8), :] = jnp.zeros((8, 128), f32)
    last = ROWS - 16
    halo_out[...] = (acc1[pl.ds(last, 16), :] * row_scale(last, 16)).astype(bf16)
    halo = pltpu.make_async_remote_copy(
        src_ref=halo_out, dst_ref=halo_in, send_sem=hsem.at[0], recv_sem=hsem.at[1],
        device_id={"ctx": lax.rem(c + 1, NC)}, device_id_type=MESH,
    )
    halo.start()

    def to_streams(i, _):
        lo = pl.multiple_of(i * 32, 32)
        block = (acc1[pl.ds(lo, 32), :] * row_scale(lo, 32)).astype(bf16)
        block = block.astype(f32)
        for k in range(6):
            strm[k, pl.ds(lo + 8, 32), :] = block[:, k * 128 : (k + 1) * 128]
        return 0

    lax.fori_loop(0, ROWS // 32, to_streams, 0)

    def tap(j, s):
        return taps[j, pl.ds(s, 1), :]

    def stream_rows(start):
        return jnp.concatenate(
            [strm[k, pl.ds(start, CHUNKS, stride=SPAN), :] for k in range(6)], axis=1
        )

    def short(now, one, two):
        out = []
        for s in range(3):
            cols = slice(s * WIDTH, (s + 1) * WIDTH)
            out.append(tap(0, s) * now[:, cols] + tap(1, s) * one[:, cols] + tap(2, s) * two[:, cols])
        return out

    def short_step(s, _):
        q, k, v = short(stream_rows(s + 8), stream_rows(s + 7), stream_rows(s + 6))
        qs[s] = q
        upad[SPAN + s] = k * v
        return 0

    lax.fori_loop(2, SPAN, short_step, 0)
    halo.wait_recv()
    before = jnp.where(c == 0, 0.0, halo_in[...].astype(f32)[8:16, :])
    for k in range(6):
        strm[k, pl.ds(0, 8), :] = before[:, k * 128 : (k + 1) * 128]
    lax.fori_loop(0, 2, short_step, 0)

    def horner(s, state):
        u = upad[SPAN + s]
        return tuple(state[n] * mode_a[pl.ds(n, 1), :] + u for n in range(MODES))

    zero = jnp.zeros((CHUNKS, WIDTH), f32)
    state = lax.fori_loop(0, SPAN, horner, (zero,) * MODES)
    sub = lax.broadcasted_iota(jnp.int32, (CHUNKS, WIDTH), 0)
    for n in range(MODES):
        e = state[n]
        for k in (1, 2, 4):
            moved = jnp.where(sub >= k, pltpu.roll(e, k, 0), 0.0)
            e = e + mode_p[n, pl.ds(k, 1), :] * moved
        e_out[pl.ds(n, 1), :] = e[CHUNKS - 1 : CHUNKS, :]
        ends[n] = jnp.where(sub >= 1, pltpu.roll(e, 1, 0), 0.0)

    def state_copy(j):
        return pltpu.make_async_remote_copy(
            src_ref=e_out, dst_ref=e_in.at[c], send_sem=es.at[j], recv_sem=er.at[c],
            device_id={"ctx": j}, device_id_type=MESH,
        )

    for j in range(1, NC):

        @pl.when(j > c)
        def _():
            state_copy(j).start()

    for block in range(SPAN // 8):

        def lag(d, total):
            return total + mode_f[d][None] * upad[pl.ds(SPAN + block * 8 - d, 8)]

        conv[pl.ds(block * 8, 8)] = lax.fori_loop(
            0, block * 8 + 8, lag, jnp.zeros((8, CHUNKS, WIDTH), f32)
        )

    whole = jnp.exp(-decay[...] * float(ROWS))

    def arrive(i, total):
        pltpu.make_async_remote_copy(
            src_ref=e_out, dst_ref=e_in.at[i], send_sem=es.at[0], recv_sem=er.at[i],
            device_id={"ctx": 0}, device_id_type=MESH,
        ).wait_recv()
        return total * whole + e_in[i]

    inward = lax.fori_loop(0, c, arrive, jnp.zeros((MODES, WIDTH), f32))
    rise = modal[...] * mode_a[...]
    begin = tuple(
        (ends[n] + inward[n : n + 1, :] * mode_p[n]) * rise[n : n + 1, :] for n in range(MODES)
    )

    def spread(t, state):
        total = conv[t]
        for n in range(MODES):
            total = total + state[n]
        gated = qs[t] * total
        for k in range(2):
            gate[k, pl.ds(t, CHUNKS, stride=SPAN), :] = gated[:, k * 128 : (k + 1) * 128]
        return tuple(state[n] * mode_a[pl.ds(n, 1), :] for n in range(MODES))

    lax.fori_loop(0, SPAN, spread, begin)
    for k in range(2):
        cols = pl.ds(k * 128, 128)
        mixed[:, cols] = (res[:, cols].astype(f32) + gate[k]).astype(bf16)

    def before_second():
        for copy in wcopies[3:]:
            copy.wait()

    gather(mixed, g2, 1, before_second, folder(again, w2s, acc2))

    def finish(i, _):
        lo = pl.multiple_of(i * 32, 32)
        rows = acc2[pl.ds(lo, 32), :] * row_scale(lo, 32)
        cosine, sine = cs[pl.ds(lo, 32), pl.ds(0, HD)], cs[pl.ds(lo, 32), pl.ds(HD, HD)]

        def turn(x):
            return (x * cosine + pltpu.roll(x, HD // 2, 1) * sine).astype(bf16)

        qrot[pl.ds(lo, 32), :] = turn(rows[:, :HD])
        kv[pl.ds(lo, 32), pl.ds(0, HD)] = turn(rows[:, HD : 2 * HD])
        kv[pl.ds(lo, 32), pl.ds(HD, HD)] = rows[:, 2 * HD :].astype(bf16)
        return 0

    lax.fori_loop(0, ROWS // 32, finish, 0)

    def kv_copy(src, org, sem, to):
        return pltpu.make_async_remote_copy(
            src_ref=src, dst_ref=kvs.at[org], send_sem=sem, recv_sem=kr.at[org],
            device_id={"ctx": to}, device_id_type=MESH,
        )

    sibling = c + sgn

    @pl.when(core == 0)
    def _():
        kv_copy(kv, c, ks.at[0], sibling).start()

    for j in range(1, NC // 2):

        @pl.when(j > chip)
        def _():
            kv_copy(kv, c, ks.at[j], 2 * j + core).start()

    factor = 1.0 / HD**0.5

    def attend(ref, diagonal, first):
        scores = (
            lax.dot_general(
                qrot[...], ref[:, pl.ds(0, HD)], (((1,), (1,)), ((), ())), preferred_element_type=f32
            )
            * factor
        )
        if diagonal:
            row = lax.broadcasted_iota(jnp.int32, scores.shape, 0)
            col = lax.broadcasted_iota(jnp.int32, scores.shape, 1)
            scores = jnp.where(col <= row, scores, -1e30)
        best = jnp.max(scores, axis=1, keepdims=True)
        if not first:
            best = jnp.maximum(best, m_s[:, pl.ds(0, 1)])
        weights = jnp.exp(scores - best)
        sums = jnp.sum(weights, axis=1, keepdims=True)
        update = jnp.dot(weights.astype(bf16), ref[:, pl.ds(HD, HD)], preferred_element_type=f32)
        if first:
            l_s[...] = jnp.broadcast_to(sums, l_s.shape)
            o_s[...] = update
        else:
            rescale = jnp.exp(m_s[...] - best)
            l_s[...] = l_s[...] * rescale + sums
            o_s[...] = o_s[...] * rescale + update
        m_s[...] = jnp.broadcast_to(best, m_s.shape)

    attend(kv, True, True)

    @pl.when(core == 1)
    def _():
        kv_copy(kv, c - 1, ks.at[0], 0).wait_recv()
        attend(kvs.at[c - 1], False, False)

    def earlier(k, _):
        org = 2 * (chip - 1 - k) + core
        other = org + sgn
        kv_copy(kv, org, ks.at[0], sibling).wait_recv()
        kv_copy(kvs.at[org], org, fs.at[k], sibling).start()
        attend(kvs.at[org], False, False)
        kv_copy(kv, other, ks.at[0], sibling).wait_recv()
        attend(kvs.at[other], False, False)
        return 0

    lax.fori_loop(0, chip, earlier, 0)
    attended[...] = (o_s[...] / l_s[...]).astype(bf16)

    for one in sends:
        one.wait_send()
    halo.wait_send()
    for j in range(1, NC):

        @pl.when(j > c)
        def _():
            state_copy(j).wait_send()

    @pl.when(core == 0)
    def _():
        kv_copy(kv, c, ks.at[0], sibling).wait_send()

    for j in range(1, NC // 2):

        @pl.when(j > chip)
        def _():
            kv_copy(kv, c, ks.at[j], 2 * j + core).wait_send()

    def passed(k, _):
        org = 2 * (chip - 1 - k) + core
        kv_copy(kvs.at[org], org, fs.at[k], sibling).wait_send()
        return 0

    lax.fori_loop(0, chip, passed, 0)


def local(residual, hyena_gain, in_weight, short_filter, decay_rate, residue, skip_gain, attn_gain, qkv_weight):
    far, near = rope_tables()
    vmem = pl.BlockSpec(memory_space=pltpu.VMEM)
    hbm = pl.BlockSpec(memory_space=pl.ANY)
    dma = pltpu.SemaphoreType.DMA
    return pl.pallas_call(
        kernel,
        out_shape=(
            jax.ShapeDtypeStruct((ROWS, WIDTH), bf16),
            jax.ShapeDtypeStruct((ROWS, HD), bf16),
        ),
        in_specs=[vmem, vmem, hbm, vmem, vmem, vmem, vmem, vmem, hbm, vmem, vmem],
        out_specs=(vmem, vmem),
        scratch_shapes=[
            pltpu.VMEM((NH, ROWS, WIDTH), bf16),
            pltpu.VMEM((NH, ROWS, WIDTH), bf16),
            pltpu.VMEM((NH * WIDTH, 3 * WIDTH), bf16),
            pltpu.VMEM((NH * WIDTH, 3 * HD), bf16),
            pltpu.VMEM((ROWS, 3 * WIDTH), f32),
            pltpu.VMEM((ROWS, 3 * HD), f32),
            pltpu.VMEM((ROWS, 128), f32),
            pltpu.VMEM((6, ROWS + 8, 128), f32),
            pltpu.VMEM((16, 3 * WIDTH), bf16),
            pltpu.VMEM((16, 3 * WIDTH), bf16),
            pltpu.VMEM((MODES, WIDTH), f32),
            pltpu.VMEM((MODES, CHUNKS, WIDTH), f32),
            pltpu.VMEM((SPAN, CHUNKS, WIDTH), f32),
            pltpu.VMEM((MODES, WIDTH), f32),
            pltpu.VMEM((2 * SPAN, CHUNKS, WIDTH), f32),
            pltpu.VMEM((SPAN, CHUNKS, WIDTH), f32),
            pltpu.VMEM((SPAN, CHUNKS, WIDTH), f32),
            pltpu.VMEM((MODES, CHUNKS, WIDTH), f32),
            pltpu.VMEM((2, ROWS, 128), f32),
            pltpu.VMEM((MODES, WIDTH), f32),
            pltpu.VMEM((NC, MODES, WIDTH), f32),
            pltpu.VMEM((ROWS, 2 * HD), f32),
            pltpu.VMEM((ROWS, HD), bf16),
            pltpu.VMEM((ROWS, 2 * HD), bf16),
            pltpu.VMEM((NC, ROWS, 2 * HD), bf16),
            pltpu.VMEM((ROWS, HD), f32),
            pltpu.VMEM((ROWS, HD), f32),
            pltpu.VMEM((ROWS, HD), f32),
            dma((6,)),
            dma((2, 32)),
            dma((2, 2, NH)),
            dma((2,)),
            dma((NC,)),
            dma((NC,)),
            dma((NC // 2,)),
            dma((NC,)),
            dma((NC // 2,)),
        ],
        compiler_params=pltpu.CompilerParams(
            collective_id=1, has_side_effects=True, vmem_limit_bytes=48 << 20
        ),
        name="genome",
    )(
        residual,
        hyena_gain.reshape(1, -1),
        in_weight.transpose(1, 0, 2),
        short_filter,
        decay_rate.T,
        residue.T,
        skip_gain.reshape(1, -1),
        attn_gain.reshape(1, -1),
        qkv_weight.transpose(1, 0, 2),
        far.reshape(NC, 1, -1),
        near,
    )


def solution(mesh):
    return jax.shard_map(
        local,
        mesh=mesh,
        in_specs=(
            P("ctx", "head"),
            P(),
            P(None, None, "head"),
            P(None, None, "head"),
            P("head", None),
            P("head", None),
            P("head"),
            P(),
            P(None, None, "head"),
        ),
        out_specs=(P("ctx", "head"), P("ctx", "head")),
        check_vma=False,
    )
```

time: 412 us -> 95.7 us (0.23)
  the two profiles are of different devices: /device:TPU:3 before, /device:TPU:19 now
where the time goes in v1:
time: 95.7 us; the launch traced here: 95.1 us
  Pallas kernels  84.4 us (88%)
  local copies, waits for them, and re-layouts  9.99 us (10%)
    pallas_call x1, Pallas kernels, local(): pl.pallas_call(kernel, out_shape=(jax.ShapeDtypeStruct((ROWS, WIDTH), bf1...  84.4 us
    unnamed x22, local copies, waits for them, and re-layouts  9.99 us

profile of v1, /device:TPU:19, one launch (start us, length us, event | category | flops | bytes accessed | tf_op | source)
XLA Modules:
  0.0 95.1 jit_solution(15942083524520030829)
XLA Ops:
  0.6 0.0 copy-start
  0.6 1.9 %copy-done = bf16[4096,3,128]{2,0,1:T(8,128)(2,1)S(1)} copy-done((bf16[4096,3,128]{2,0,1:T(8,128)(2,1)S(1)}, bf16[4096,3,128]{2,0,1:T(8,128)(2,1)}, u32[]{:S(2)}) %copy-start) | copy-done | bytes 3145752
  2.5 0.0 copy-start.1
  2.5 0.9 copy-done.1
  3.5 0.0 copy-start.2
  3.5 0.9 copy-done.2
  4.4 0.0 copy-start.3
  4.4 0.7 copy-done.3
  5.1 0.0 copy-start.4
  5.1 0.7 copy-done.4
  5.8 0.0 copy-start.5
  5.8 0.7 copy-done.5
  6.5 0.0 copy-start.6
  6.5 0.7 copy-done.6
  7.3 0.0 copy-start.7
  7.3 0.7 copy-done.7
  8.0 0.0 copy-start.8
  8.0 0.7 copy-done.8
  8.7 0.0 copy-start.9
  8.7 0.7 copy-done.9
  9.4 84.4 %genome.1 = (bf16[256,256]{1,0:T(8,128)(2,1)S(1)}, bf16[256,128]{1,0:T(8,128)(2,1)S(1)}) custom-call(bf16[256,256]{1,0:T(8,128)(2,1)S(1)} %copy-done.2, f32[1,4096]{1,0:T(1,128)S(1)} %bitcast.8, bf16[3,4096,256]{2,1,0:T(8,128)(2,1)} %bitcast.13, f32[3,3,256]{2,1,0:T(4,128)S(1)} %copy-done.8, f32[16,256]{1,0:T(8,128)S(1)} %bitcast.9, f32[16,256]{1,0:T(8,128)S(1)} %bitcast.10, ...), custom_call_target="tpu_custom_call" | custom-call | tf_op jit(solution)/shard_map/genome/pallas_call | solution.py:441
  93.8 0.7 copy.15
  94.5 0.6 copy.16
Async XLA Ops:
  0.6 1.9 %copy-start = (bf16[4096,3,128]{2,0,1:T(8,128)(2,1)S(1)}, bf16[4096,3,128]{2,0,1:T(8,128)(2,1)}, u32[]{:S(2)}) copy-start(bf16[4096,3,128]{2,0,1:T(8,128)(2,1)} %param.19) | copy-start | bytes 9437188
  2.5 0.9 copy-start.1
  3.5 0.9 copy-start.2
  4.4 0.7 copy-start.3
  5.1 0.7 copy-start.4
  5.8 0.7 copy-start.5
  6.5 0.7 copy-start.6
  7.3 0.7 copy-start.7
  8.0 0.7 copy-start.8
  8.7 0.7 copy-start.9

commit v2 on v1

v2 whole, which is shorter than its diff:
```python
import functools

import jax
import jax.numpy as jnp
import numpy as np
from jax import lax
from jax.experimental import pallas as pl
from jax.experimental.pallas import tpu as pltpu
from jax.sharding import PartitionSpec as P

MESH = pl.DeviceIdType.MESH
f32 = jnp.float32
bf16 = jnp.bfloat16

HD = 128
EPS = 1e-6
ROWS = 256
WIDTH = 256
NH = 16
NC = 16
NZ = 8
MODES = 16
SPAN = 32
CHUNKS = 8
STOP = 9
NOATT = 0
TREE = (0, 1)
DESC = 1
UN = 4
LAG0 = 8
LAG1 = 3
NOFOLD = 0
DIST = 4
PARTS1 = (((0, 80, 0), (80, 48, 1), (128, 80, 0), (208, 48, 1)),)
PARTS2 = (((0, 80, 0), (80, 48, 1)), ((128, 80, 0), (208, 48, 1)))
GROUP = 128
KVORDER = 1


def rope_tables():
    half = HD // 2
    inverse = 10000.0 ** (-np.arange(half) / half)

    def table(positions):
        angle = positions[:, None] * inverse[None, :]
        cos, sin = np.cos(angle), np.sin(angle)
        return np.concatenate([cos, cos, sin, sin], axis=1).astype(np.float32)

    return table(np.arange(NC) * float(ROWS)), table(np.arange(ROWS) * 1.0)


def kernel(
    res_h, hgain_h, w1, taps_h, decay_h, residue_h, skip_h, again_h, w2, far_h, near_h,
    mixed, attended,
    hgain, taps, decay, residue, skip, again, far, near,
    g1, g2, w1s, w2s, acc1, acc2, sq, strm, halo_out, halo_in,
    mode_a, mode_b, mode_p, mode_f, modal, upad, qs, conv, ends, gate, e_out, e_in, s_out, s_in,
    cs, qt, kv, kvs, m_s, l_s, o_s, att,
    psem, osem, asem, wsem, gs, gr, hsem, ssem, es, er, ks, kr, fs, rs,
):
    c = lax.axis_index("ctx")
    h = lax.axis_index("head")
    core = lax.rem(c, 2)
    sgn = 1 - 2 * core
    z = lax.rem(h, NZ)
    xh = h // NZ
    chip = c // 2

    def head(x, zz):
        return x * NZ + lax.rem(zz + 2 * NZ, NZ)

    partner = head(1 - xh, z)
    ahead = head(xh, z + sgn)
    behind = head(xh, z - sgn)

    small = ((res_h, g1.at[h]), (decay_h, decay), (residue_h, residue), (skip_h, skip), (hgain_h, hgain),
             (taps_h, taps), (far_h, far), (near_h, near), (again_h, again))
    scopies = [pltpu.make_async_copy(a, b, psem.at[k]) for k, (a, b) in enumerate(small)]
    for copy in scopies:
        copy.start()
    wcopies = []
    for j in range(3):
        wcopies.append(pltpu.make_async_copy(w1.at[j], w1s.at[:, pl.ds(j * WIDTH, WIDTH)], wsem.at[j]))
    for j in range(3):
        wcopies.append(pltpu.make_async_copy(w2.at[j], w2s.at[:, pl.ds(j * HD, HD)], wsem.at[3 + j]))
    for copy in wcopies:
        copy.start()

    barrier = pltpu.get_barrier_semaphore()
    slant, slant_back = head(1 - xh, z + sgn), head(1 - xh, z - sgn)
    for to in (partner, ahead, behind, slant, slant_back):
        pl.semaphore_signal(barrier, inc=1, device_id={"head": to}, device_id_type=MESH)
    for k in range(1, NC // 2):
        to = 2 * lax.rem(chip + k, NC // 2) + core
        pl.semaphore_signal(barrier, inc=1, device_id={"ctx": to}, device_id_type=MESH)
    for k in (1, NC - 1):
        pl.semaphore_signal(
            barrier, inc=1, device_id={"ctx": lax.rem(c + k, NC)}, device_id_type=MESH
        )
    pl.semaphore_wait(barrier, 5 + NC // 2 - 1 + 2)
    scopies[0].wait()


    def gather(g, which, groups, prepare, fold, done):
        numbers, count = [], 0
        for group in groups:
            numbers.append(range(count, count + len(group)))
            count += len(group)
        flat = [part for group in groups for part in group]

        def copy(p, org, to):
            rows = g.at[org, pl.ds(flat[p][0], flat[p][1])]
            return pltpu.make_async_remote_copy(
                src_ref=rows, dst_ref=rows, send_sem=gs.at[which, p], recv_sem=gr.at[which, p, org],
                device_id={"head": to}, device_id_type=MESH,
            )

        def send(p, org, to):
            copy(p, org, to).start()

        def wait(p, org):
            copy(p, org, partner).wait_recv()

        def begin(n):
            for p in numbers[n]:
                if flat[p][2]:
                    send(p, h, slant)
                    send(p, h, slant_back)
            for p in numbers[n]:
                send(p, h, ahead)
                send(p, h, behind)
            for p in numbers[n]:
                send(p, h, partner)

        def step(n, d, between=lambda j: None):
            a, b = head(xh, z - sgn * d), head(xh, z + sgn * d)
            a2, b2 = head(1 - xh, z - sgn * d), head(1 - xh, z + sgn * d)

            def hop(p, org, to, far, over):
                wait(p, org)

                @pl.when(d < far)
                def _():
                    send(p, org, to)
                    if over and far == 3:
                        send(p, org, partner)

                if over and far == 3:

                    @pl.when(d == 3)
                    def _():
                        send(p, org, partner)

                if over and far == 4:

                    @pl.when(d == 3)
                    def _():
                        send(p, org, slant)

                    @pl.when(d < 4)
                    def _():
                        send(p, org, partner)

            def both(p, first, second, to, back, over):
                hop(p, first, to, 4, over)

                @pl.when(d < 4)
                def _():
                    hop(p, second, back, 3, over)

            calls = [(p, a, b, ahead, behind, not flat[p][2]) for p in numbers[n]]
            calls += [(p, b2, a2, behind, ahead, False) for p in numbers[n] if flat[p][2]]
            for i, call in enumerate(calls):
                both(*call)
                for j in range(4 * i // len(calls), 4 * (i + 1) // len(calls)):
                    between(j)

        def folds(n, d):
            def one(j):
                over = j >= jnp.where(d == 1, 3, jnp.where(d == 4, 1, 2))
                here = jnp.where(d == 1, j, 2 * d - 1 + j)
                there = jnp.where(d == 1, 0, jnp.where(d == 4, 4 + j, 2 * d - 5 + j))
                k = jnp.where(over, there, here)
                apart = jnp.where(k % 2 == 1, -((k + 1) // 2), k // 2)
                org = head(jnp.where(over, 1 - xh, xh), z + sgn * apart)

                @pl.when(over)
                def _():
                    for p in numbers[n]:
                        if not flat[p][2]:
                            wait(p, org)

                @pl.when(jnp.logical_and(over, k == 0))
                def _():
                    for p in numbers[n]:
                        if flat[p][2]:
                            wait(p, org)

                if not NOFOLD:
                    fold(groups[n], org)

            return one

        def all_folds(n, d):
            one = folds(n, d)

            def body(j, _):
                one(j)
                return 0

            lax.fori_loop(0, 4, body, 0)

        lag = len(groups) > 1
        for n in range(len(groups)):
            begin(n)
        step(0, 1)
        prepare()

        def later(d, _):
            step(0, d, folds(0, d - 1))
            if lag:
                step(1, d - 1)

                @pl.when(d > 2)
                def _():
                    all_folds(1, d - 2)

            return 0

        lax.fori_loop(2, 5, later, 0)
        all_folds(0, 4)
        done(0)
        if lag:
            all_folds(1, 3)
            step(1, 4)
            all_folds(1, 4)
            done(1)

    def sent(g, which, groups):
        for p, part in enumerate(part for group in groups for part in group):
            rows = g.at[pl.ds(0, NH - 1), pl.ds(part[0], part[1])]
            pltpu.make_async_remote_copy(
                src_ref=rows, dst_ref=rows, send_sem=gs.at[which, p], recv_sem=gr.at[which, p, 0],
                device_id={"head": partner}, device_id_type=MESH,
            ).wait_send()

    def folder(g, gain, w, acc):
        def fold(group, org):
            lo, n = group[0][0], sum(part[1] for part in group)
            here = pl.ds(lo, n)
            columns = pl.ds(pl.multiple_of(org * WIDTH, WIDTH), WIDTH)
            rows = g[org, here].astype(f32)
            squares = rows * rows
            sq[here, :] += squares[:, :128] + squares[:, 128:]
            scaled = (rows * gain[:, columns]).astype(bf16)
            acc[here, :] += jnp.dot(scaled, w[columns, :], preferred_element_type=f32)

        return fold

    def row_scale(lo, n):
        total = jnp.sum(sq[pl.ds(lo, n), :], axis=1, keepdims=True)
        return lax.rsqrt(total * (1.0 / (NH * WIDTH)) + EPS)

    def tables():
        d = decay[...]
        a = jnp.exp(-d)
        mode_a[...] = a
        twice = 2.0 * d
        series = twice * (1.0 - twice * (0.5 - twice * (1.0 / 6 - twice * (1.0 / 24 - twice * (1.0 / 120)))))
        coef = residue[...] * jnp.sqrt(jnp.where(twice < 0.1, series, 1.0 - jnp.exp(-twice)))
        modal[...] = coef
        steps = lax.broadcasted_iota(jnp.int32, (CHUNKS, WIDTH), 0).astype(f32)
        for n in range(MODES):
            mode_b[n] = jnp.broadcast_to(mode_a[pl.ds(n, 1), :], (CHUNKS, WIDTH))
            mode_p[n] = jnp.exp(-decay[pl.ds(n, 1), :] * (steps * SPAN))
        lags = lax.broadcasted_iota(jnp.int32, (SPAN, WIDTH), 0).astype(f32)
        filt = jnp.zeros((SPAN, WIDTH), f32)
        for n in range(MODES):
            filt = filt + modal[pl.ds(n, 1), :] * jnp.exp(-decay[pl.ds(n, 1), :] * lags)
        filt = filt + jnp.where(lags == 0.0, skip[...], 0.0)
        for t in range(SPAN):
            mode_f[t] = jnp.broadcast_to(filt[t : t + 1, :], (CHUNKS, WIDTH))
        upad[pl.ds(0, SPAN)] = jnp.zeros((SPAN, CHUNKS, WIDTH), f32)
        there = far[c]
        fc, fsn = there[:, :HD], there[:, HD:]
        nc, ns = near[:, pl.ds(0, HD)], near[:, pl.ds(HD, HD)]
        cs[:, pl.ds(0, HD)] = nc * fc - ns * fsn
        lane = lax.broadcasted_iota(jnp.int32, (ROWS, HD), 1)
        sine = ns * fc + nc * fsn
        cs[:, pl.ds(HD, HD)] = jnp.where(lane < HD // 2, -sine, sine)

    def before_first():
        for copy in scopies[1:]:
            copy.wait()
        tables()
        sq[...] = jnp.zeros_like(sq)
        acc1[...] = jnp.zeros_like(acc1)
        for copy in wcopies[:3]:
            copy.wait()

    if STOP < 1:
        before_first()
    if STOP >= 1:
        gather(g1, 0, PARTS1, before_first, folder(g1, hgain, w1s, acc1), lambda n: None)

    if STOP >= 2:
        last = ROWS - 16
        halo_out[...] = (acc1[pl.ds(last, 16), :] * row_scale(last, 16)).astype(bf16)
        halo = pltpu.make_async_remote_copy(
            src_ref=halo_out, dst_ref=halo_in, send_sem=hsem.at[0], recv_sem=hsem.at[1],
            device_id={"ctx": lax.rem(c + 1, NC)}, device_id_type=MESH,
        )
        halo.start()
        for k in range(6):
            strm[k, pl.ds(0, 8), :] = jnp.zeros((8, 128), f32)

        def to_streams(i, _):
            lo = pl.multiple_of(i * 32, 32)
            block = (acc1[pl.ds(lo, 32), :] * row_scale(lo, 32)).astype(bf16)
            block = block.astype(f32)
            for k in range(6):
                strm[k, pl.ds(lo + 8, 32), :] = block[:, k * 128 : (k + 1) * 128]
            return 0

        lax.fori_loop(0, ROWS // 32, to_streams, 0)

        def tap(j, s):
            return taps[j, pl.ds(s, 1), :]

        def stream_rows(start):
            return jnp.concatenate(
                [strm[k, pl.ds(start, CHUNKS, stride=SPAN), :] for k in range(6)], axis=1
            )

        def short(now, one, two):
            out = []
            for s in range(3):
                cols = slice(s * WIDTH, (s + 1) * WIDTH)
                out.append(tap(0, s) * now[:, cols] + tap(1, s) * one[:, cols] + tap(2, s) * two[:, cols])
            return out

        def short_step(s, _):
            q, k, v = short(stream_rows(s + 8), stream_rows(s + 7), stream_rows(s + 6))
            qs[s] = q
            upad[SPAN + s] = k * v
            return 0

        lax.fori_loop(0, SPAN, short_step, 0, unroll=UN)

    if STOP >= 3:
        def horner(s, state):
            u = upad[SPAN + s]
            return tuple(state[n] * mode_b[n] + u for n in range(MODES))

        zero = jnp.zeros((CHUNKS, WIDTH), f32)
        state = lax.fori_loop(0, SPAN, horner, (zero,) * MODES, unroll=UN)
        sub = lax.broadcasted_iota(jnp.int32, (CHUNKS, WIDTH), 0)
        for n in range(MODES):
            e = state[n]
            for k in (1, 2, 4):
                moved = jnp.where(sub >= k, pltpu.roll(e, k, 0), 0.0)
                e = e + mode_p[n, pl.ds(k, 1), :] * moved
            e_out[pl.ds(n, 1), :] = e[CHUNKS - 1 : CHUNKS, :]
            ends[n] = jnp.where(sub >= 1, pltpu.roll(e, 1, 0), 0.0)

        def inside(block):
            def lag(d, total):
                return total + mode_f[d][None] * upad[pl.ds(SPAN + block * 8 - d, 8)]

            conv[pl.ds(block * 8, 8)] = lax.fori_loop(
                0, block * 8 + 8, lag, jnp.zeros((8, CHUNKS, WIDTH), f32), unroll=UN
            )

        for block in range(3):
            inside(block)

        halo.wait_recv()
        before = jnp.where(c == 0, 0.0, halo_in[...].astype(f32)[14:16, :])
        first, second = [], []
        for s in range(3):
            two, one = (before[r : r + 1, s * WIDTH : (s + 1) * WIDTH] for r in range(2))
            now, then = (
                jnp.concatenate([strm[2 * s + k, pl.ds(8 + r, 1), :] for k in range(2)], axis=1)
                for r in range(2)
            )
            base = tap(0, s) * now
            first.append((base, tap(1, s) * one + tap(2, s) * two))
            base = tap(0, s) * then + tap(1, s) * now
            second.append((base, tap(2, s) * one))

        def product(pair):
            (k, dk), (v, dv) = pair[1:]
            return k * dv + dk * v + dk * dv

        du0, du1 = product(first), product(second)
        inverse = jnp.exp(decay[...])
        come = (du0 + du1 * inverse) * inverse
        whole = jnp.exp(-decay[...] * float(ROWS))
        e_out[...] += whole * come

        def state_copy(j):
            return pltpu.make_async_remote_copy(
                src_ref=e_out, dst_ref=e_in.at[chip], send_sem=es.at[j], recv_sem=er.at[chip],
                device_id={"ctx": 2 * j + core}, device_id_type=MESH,
            )

        for j in range(1, NC // 2):

            @pl.when(j > chip)
            def _():
                state_copy(j).start()

        inside(3)
        qs[0, pl.ds(0, 1), :] += first[0][1]
        qs[1, pl.ds(0, 1), :] += second[0][1]
        early = jnp.sum(modal[...] * inverse, axis=0, keepdims=True)
        conv[0, pl.ds(0, 1), :] += skip[...] * du0 - early * du1
        conv[1, pl.ds(0, 1), :] += skip[...] * du1
        double = whole * whole

        def arrive(i, total):
            pltpu.make_async_remote_copy(
                src_ref=e_out, dst_ref=e_in.at[i], send_sem=es.at[0], recv_sem=er.at[i],
                device_id={"ctx": c + sgn}, device_id_type=MESH,
            ).wait_recv()
            return total * double + e_in[i]

        same = lax.fori_loop(0, chip, arrive, jnp.zeros((MODES, WIDTH), f32))
        s_out[...] = jnp.where(core == 0, whole * (whole * same) + e_out[...], same)
        swap = pltpu.make_async_remote_copy(
            src_ref=s_out, dst_ref=s_in, send_sem=ssem.at[0], recv_sem=ssem.at[1],
            device_id={"ctx": c + sgn}, device_id_type=MESH,
        )
        swap.start()
        rise = modal[...] * mode_a[...]
        swap.wait_recv()
        inward = whole * same + s_in[...] + come
        begin = tuple(
            (ends[n] + inward[n : n + 1, :] * mode_p[n]) * rise[n : n + 1, :] for n in range(MODES)
        )

        def spread(t, state):
            total = conv[t]
            for n in range(MODES):
                total = total + state[n]
            gated = qs[t] * total
            for k in range(2):
                gate[k, pl.ds(t, CHUNKS, stride=SPAN), :] = gated[:, k * 128 : (k + 1) * 128]
            return tuple(state[n] * mode_b[n] for n in range(MODES))

        lax.fori_loop(0, SPAN, spread, begin, unroll=UN)
        for k in range(2):
            cols = pl.ds(k * 128, 128)
            g2[h, :, cols] = (g1[h, :, cols].astype(f32) + gate[k]).astype(bf16)

    if STOP >= 4:
        out_copy = pltpu.make_async_copy(g2.at[h], mixed, osem)
        out_copy.start()

        def kv_copy(src, org, n, sem, to):
            return pltpu.make_async_remote_copy(
                src_ref=src, dst_ref=kvs.at[org, n], send_sem=sem, recv_sem=kr.at[org, n],
                device_id={"ctx": to}, device_id_type=MESH,
            )

        sibling = c + sgn

        half = NC // 4

        def kv_goes(j, n):
            if j < half or not TREE[n]:
                return j > chip
            return jnp.logical_or(j == chip + half, jnp.logical_and(j > chip, chip >= half))

        def relay_copy(j, n):
            org = c - 2 * half
            return kv_copy(kvs.at[org, n], org, n, rs.at[j - half, n], 2 * j + core)

        def relay(n):
            @pl.when(jnp.logical_and(chip >= half, TREE[n] == 1))
            def _():
                relay_copy(half, n).wait_recv()
                for j in range(half, 2 * half):

                    @pl.when(j != chip)
                    def _():
                        relay_copy(j, n).start()

        def finish(n):
            lo = n * GROUP
            here = pl.ds(lo, GROUP)
            rows = acc2[here, :] * row_scale(lo, GROUP)
            cosine, sine = cs[here, pl.ds(0, HD)], cs[here, pl.ds(HD, HD)]

            def turn(x):
                return x * cosine + pltpu.roll(x, HD // 2, 1) * sine

            kv[n, :, pl.ds(0, HD)] = turn(rows[:, HD : 2 * HD]).astype(bf16)
            kv[n, :, pl.ds(HD, HD)] = rows[:, 2 * HD :].T.astype(bf16)
            if STOP >= 5:
                for k in range(1, NC // 2):
                    j = NC // 2 - k if DESC else k

                    @pl.when(kv_goes(j, n))
                    def _(j=j):
                        kv_copy(kv.at[n], c, n, ks.at[j, n], 2 * j + core).start()

                @pl.when(core == 0)
                def _():
                    kv_copy(kv.at[n], c, n, ks.at[0, n], sibling).start()

            qt[:, here] = turn(rows[:, :HD]).T.astype(bf16)

        def before_second():
            sq[...] = jnp.zeros_like(sq)
            acc2[...] = jnp.zeros_like(acc2)
            for copy in wcopies[3:]:
                copy.wait()

        def finished(n):
            if len(PARTS2) > 1:
                finish(n)
            else:
                finish(0)
                finish(1)

            if STOP >= 5 and n == 1:
                relay(0)

        gather(g2, 1, PARTS2, before_second, folder(g2, again, w2s, acc2), finished)

    if STOP >= 5:
        factor = 1.0 / HD**0.5

        def attend(refs, diagonal):
            keys = jnp.concatenate([ref[:, pl.ds(0, HD)] for ref in refs], axis=0)
            scores = jnp.dot(keys, qt[...], preferred_element_type=f32) * factor
            if diagonal:
                key = lax.broadcasted_iota(jnp.int32, scores.shape, 0)
                query = lax.broadcasted_iota(jnp.int32, scores.shape, 1)
                scores = jnp.where(key <= query, scores, -1e30)
            best = jnp.max(scores, axis=0, keepdims=True)
            if not diagonal:
                best = jnp.maximum(best, m_s[...])
            weights = jnp.exp(scores - best)
            sums = jnp.sum(weights, axis=0, keepdims=True)
            values = jnp.concatenate([ref[:, pl.ds(HD, HD)] for ref in refs], axis=1)
            update = jnp.dot(values, weights.astype(bf16), preferred_element_type=f32)
            if diagonal:
                l_s[...] = sums
                o_s[...] = update
            else:
                rescale = jnp.exp(m_s[...] - best)
                l_s[...] = l_s[...] * rescale + sums
                o_s[...] = o_s[...] * rescale + update
            m_s[...] = best

        def origin(k):
            return 2 * (chip - 1 - k) + core

        def pass_on(k, n):
            org = origin(k)

            @pl.when(jnp.logical_or(org != c - 2 * half, TREE[n] == 0))
            def _():
                kv_copy(kv.at[n], org, n, ks.at[0, n], sibling).wait_recv()

            kv_copy(kvs.at[org, n], org, n, fs.at[k, n], sibling).start()

        def both_cores(k, n):
            org = origin(k)
            other = org + sgn
            kv_copy(kv.at[n], other, n, ks.at[0, n], sibling).wait_recv()
            if not NOATT:
                attend((kvs.at[org, n], kvs.at[other, n]), False)

        attend((kv.at[0], kv.at[1]), True)
        relay(1)

        @pl.when(core == 1)
        def _():
            for n in range(2):
                kv_copy(kv.at[n], c - 1, n, ks.at[0, n], 0).wait_recv()
            attend((kvs.at[c - 1, 0], kvs.at[c - 1, 1]), False)

        for n in range(2):
            lag = (LAG0, LAG1)[n]

            def lagged(k, _):
                @pl.when(k < chip)
                def _():
                    pass_on(k, n)

                @pl.when(k >= lag)
                def _():
                    both_cores(k - lag, n)

                return 0

            lax.fori_loop(0, jnp.where(chip > 0, chip + lag, 0), lagged, 0)

        att[...] = (o_s[...] / l_s[...]).T.astype(bf16)
        att_copy = pltpu.make_async_copy(att, attended, asem)
        att_copy.start()

    if STOP < 4:
        for copy in wcopies[3:]:
            copy.wait()
    if STOP >= 1:
        sent(g1, 0, PARTS1)
    if STOP >= 4:
        sent(g2, 1, PARTS2)
        out_copy.wait()
    if STOP >= 5:
        att_copy.wait()
    if STOP >= 2:
        halo.wait_send()
    if STOP == 2:
        halo.wait_recv()
    if STOP >= 3:
        swap.wait_send()
        for j in range(1, NC // 2):

            @pl.when(j > chip)
            def _():
                state_copy(j).wait_send()

    if STOP >= 5:
        for n in range(2):

            @pl.when(core == 0)
            def _():
                kv_copy(kv.at[n], c, n, ks.at[0, n], sibling).wait_send()

            for j in range(1, NC // 2):

                @pl.when(kv_goes(j, n))
                def _():
                    kv_copy(kv.at[n], c, n, ks.at[j, n], 2 * j + core).wait_send()

            for j in range(half, 2 * half):

                @pl.when(jnp.logical_and(chip >= half, j != chip) if TREE[n] else False)
                def _():
                    relay_copy(j, n).wait_send()

            def passed(k, _):
                org = origin(k)
                kv_copy(kvs.at[org, n], org, n, fs.at[k, n], sibling).wait_send()
                return 0

            lax.fori_loop(0, chip, passed, 0)


def local(residual, hyena_gain, in_weight, short_filter, decay_rate, residue, skip_gain, attn_gain, qkv_weight):
    far, near = rope_tables()
    vmem = pl.BlockSpec(memory_space=pltpu.VMEM)
    hbm = pl.BlockSpec(memory_space=pltpu.MemorySpace.HBM)
    dma = pltpu.SemaphoreType.DMA
    return pl.pallas_call(
        kernel,
        out_shape=(
            jax.ShapeDtypeStruct((ROWS, WIDTH), bf16),
            jax.ShapeDtypeStruct((ROWS, HD), bf16),
        ),
        in_specs=[hbm] * 11,
        out_specs=(hbm, hbm),
        scratch_shapes=[
            pltpu.VMEM((1, NH * WIDTH), f32),
            pltpu.VMEM((3, 3, WIDTH), f32),
            pltpu.VMEM((MODES, WIDTH), f32),
            pltpu.VMEM((MODES, WIDTH), f32),
            pltpu.VMEM((1, WIDTH), f32),
            pltpu.VMEM((1, NH * WIDTH), f32),
            pltpu.VMEM((NC, 1, 2 * HD), f32),
            pltpu.VMEM((ROWS, 2 * HD), f32),
            pltpu.VMEM((NH, ROWS, WIDTH), bf16),
            pltpu.VMEM((NH, ROWS, WIDTH), bf16),
            pltpu.VMEM((NH * WIDTH, 3 * WIDTH), bf16),
            pltpu.VMEM((NH * WIDTH, 3 * HD), bf16),
            pltpu.VMEM((ROWS, 3 * WIDTH), f32),
            pltpu.VMEM((ROWS, 3 * HD), f32),
            pltpu.VMEM((ROWS, 128), f32),
            pltpu.VMEM((6, ROWS + 8, 128), f32),
            pltpu.VMEM((16, 3 * WIDTH), bf16),
            pltpu.VMEM((16, 3 * WIDTH), bf16),
            pltpu.VMEM((MODES, WIDTH), f32),
            pltpu.VMEM((MODES, CHUNKS, WIDTH), f32),
            pltpu.VMEM((MODES, CHUNKS, WIDTH), f32),
            pltpu.VMEM((SPAN, CHUNKS, WIDTH), f32),
            pltpu.VMEM((MODES, WIDTH), f32),
            pltpu.VMEM((2 * SPAN, CHUNKS, WIDTH), f32),
            pltpu.VMEM((SPAN, CHUNKS, WIDTH), f32),
            pltpu.VMEM((SPAN, CHUNKS, WIDTH), f32),
            pltpu.VMEM((MODES, CHUNKS, WIDTH), f32),
            pltpu.VMEM((2, ROWS, 128), f32),
            pltpu.VMEM((MODES, WIDTH), f32),
            pltpu.VMEM((NC // 2, MODES, WIDTH), f32),
            pltpu.VMEM((MODES, WIDTH), f32),
            pltpu.VMEM((MODES, WIDTH), f32),
            pltpu.VMEM((ROWS, 2 * HD), f32),
            pltpu.VMEM((HD, ROWS), bf16),
            pltpu.VMEM((2, GROUP, 2 * HD), bf16),
            pltpu.VMEM((NC, 2, GROUP, 2 * HD), bf16),
            pltpu.VMEM((1, ROWS), f32),
            pltpu.VMEM((1, ROWS), f32),
            pltpu.VMEM((HD, ROWS), f32),
            pltpu.VMEM((ROWS, HD), bf16),
            dma((9,)),
            dma,
            dma,
            dma((6,)),
            dma((2, 8)),
            dma((2, 8, NH)),
            dma((2,)),
            dma((2,)),
            dma((NC,)),
            dma((NC,)),
            dma((NC // 2, 2)),
            dma((NC, 2)),
            dma((NC // 2, 2)),
            dma((NC // 4, 2)),
        ],
        compiler_params=pltpu.CompilerParams(
            collective_id=1, has_side_effects=True, vmem_limit_bytes=56 << 20
        ),
        name="genome",
    )(
        residual,
        hyena_gain.reshape(1, -1),
        in_weight.transpose(1, 0, 2),
        short_filter,
        decay_rate.T,
        residue.T,
        skip_gain.reshape(1, -1),
        attn_gain.reshape(1, -1),
        qkv_weight.transpose(1, 0, 2),
        far.reshape(NC, 1, -1),
        near,
    )


def solution(mesh):
    return jax.shard_map(
        local,
        mesh=mesh,
        in_specs=(
            P("ctx", "head"),
            P(),
            P(None, None, "head"),
            P(None, None, "head"),
            P("head", None),
            P("head", None),
            P("head"),
            P(),
            P(None, None, "head"),
        ),
        out_specs=(P("ctx", "head"), P("ctx", "head")),
        check_vma=False,
    )
```

time: 95.7 us -> 79.5 us (0.83)
  the two profiles are of different devices: /device:TPU:19 before, /device:TPU:3 now
where the time goes in v2:
time: 79.5 us; the launch traced here: 79.4 us
  Pallas kernels  75.7 us (95%)
  local copies, waits for them, and re-layouts  3.04 us (4%)
    pallas_call x1, Pallas kernels, local(): pl.pallas_call(kernel, out_shape=(jax.ShapeDtypeStruct((ROWS, WIDTH), bf1...  75.7 us
    unnamed x2, local copies, waits for them, and re-layouts  3.04 us

profile of v2, /device:TPU:3, one launch (start us, length us, event | category | flops | bytes accessed | tf_op | source)
XLA Modules:
  0.0 79.4 jit_solution(16889820409274810433)
XLA Ops:
  0.6 75.7 %genome.1 = (bf16[256,256]{1,0:T(8,128)(2,1)}, bf16[256,128]{1,0:T(8,128)(2,1)}) custom-call(bf16[256,256]{1,0:T(8,128)(2,1)} %res_h.1, f32[1,4096]{1,0:T(1,128)} %bitcast.9, bf16[3,4096,256]{2,1,0:T(8,128)(2,1)} %bitcast.7, f32[3,3,256]{2,1,0:T(4,128)} %taps_h.1, f32[16,256]{1,0:T(8,128)} %bitcast.10, f32[16,256]{1,0:T(8,128)} %bitcast.11, ...), custom_call_target="tpu_custom_call" | custom-call | tf_op jit(solution)/shard_map/genome/pallas_call | solution.py:660
  76.3 1.6 %copy.15 = bf16[256,256]{1,0:T(8,128)(2,1)} copy(bf16[256,256]{1,0:T(8,128)(2,1)} %get-tuple-element.4) | data formatting | bytes 262144
  77.9 1.5 %copy.16 = bf16[256,128]{1,0:T(8,128)(2,1)} copy(bf16[256,128]{1,0:T(8,128)(2,1)} %get-tuple-element.5) | data formatting | bytes 131072

commit v3 on v2

--- a/solution.py
+++ b/solution.py
@@ -201,14 +201,26 @@
 
             return one
 
-        def all_folds(n, d):
+        def some_folds(n, d, lo, hi):
             one = folds(n, d)
 
             def body(j, _):
                 one(j)
                 return 0
 
-            lax.fori_loop(0, 4, body, 0)
+            lax.fori_loop(lo, hi, body, 0)
+
+        def final(n):
+            a, b2 = head(xh, z + 4), head(1 - xh, z + 4)
+            for p in numbers[n]:
+                wait(p, a)
+            some_folds(n, 3, 0, 4)
+            some_folds(n, 4, 0, 3)
+            for p in numbers[n]:
+                if flat[p][2]:
+                    wait(p, b2)
+            some_folds(n, 4, 3, 4)
+            done(n)
 
         lag = len(groups) > 1
         for n in range(len(groups)):
@@ -223,18 +235,17 @@
 
                 @pl.when(d > 2)
                 def _():
-                    all_folds(1, d - 2)
+                    some_folds(1, d - 2, 0, 4)
 
             return 0
 
-        lax.fori_loop(2, 5, later, 0)
-        all_folds(0, 4)
-        done(0)
+        lax.fori_loop(2, 4, later, 0)
         if lag:
-            all_folds(1, 3)
-            step(1, 4)
-            all_folds(1, 4)
-            done(1)
+            step(1, 3)
+        final(0)
+        if lag:
+            some_folds(1, 2, 0, 4)
+            final(1)
 
     def sent(g, which, groups):
         for p, part in enumerate(part for group in groups for part in group):
@@ -339,13 +350,15 @@
                 out.append(tap(0, s) * now[:, cols] + tap(1, s) * one[:, cols] + tap(2, s) * two[:, cols])
             return out
 
-        def short_step(s, _):
-            q, k, v = short(stream_rows(s + 8), stream_rows(s + 7), stream_rows(s + 6))
+        def short_step(s, rows):
+            one, two = rows
+            now = stream_rows(s + 8)
+            q, k, v = short(now, one, two)
             qs[s] = q
             upad[SPAN + s] = k * v
-            return 0
-
-        lax.fori_loop(0, SPAN, short_step, 0, unroll=UN)
+            return now, one
+
+        lax.fori_loop(0, SPAN, short_step, (stream_rows(7), stream_rows(6)), unroll=UN)
 
     if STOP >= 3:
         def horner(s, state):
@@ -528,6 +541,37 @@
                 relay(0)
 
         gather(g2, 1, PARTS2, before_second, folder(g2, again, w2s, acc2), finished)
+
+    def settle():
+        if STOP >= 1:
+            sent(g1, 0, PARTS1)
+        if STOP >= 2:
+            halo.wait_send()
+        if STOP == 2:
+            halo.wait_recv()
+        if STOP >= 3:
+            swap.wait_send()
+            for j in range(1, NC // 2):
+
+                @pl.when(j > chip)
+                def _():
+                    state_copy(j).wait_send()
+
+        if STOP >= 4:
+            sent(g2, 1, PARTS2)
+            out_copy.wait()
+        if STOP >= 5:
+            for n in range(2):
+
+                @pl.when(core == 0)
+                def _():
+                    kv_copy(kv.at[n], c, n, ks.at[0, n], sibling).wait_send()
+
+                for j in range(1, NC // 2):
+
+                    @pl.when(kv_goes(j, n))
+                    def _():
+                        kv_copy(kv.at[n], c, n, ks.at[j, n], 2 * j + core).wait_send()
 
     if STOP >= 5:
         factor = 1.0 / HD**0.5
@@ -584,6 +628,8 @@
             attend((kvs.at[c - 1, 0], kvs.at[c - 1, 1]), False)
 
         for n in range(2):
+            if n == 1:
+                settle()
             lag = (LAG0, LAG1)[n]
 
             def lagged(k, _):
@@ -603,41 +649,13 @@
         att_copy = pltpu.make_async_copy(att, attended, asem)
         att_copy.start()
 
-    if STOP < 4:
-        for copy in wcopies[3:]:
-            copy.wait()
-    if STOP >= 1:
-        sent(g1, 0, PARTS1)
-    if STOP >= 4:
-        sent(g2, 1, PARTS2)
-        out_copy.wait()
-    if STOP >= 5:
-        att_copy.wait()
-    if STOP >= 2:
-        halo.wait_send()
-    if STOP == 2:
-        halo.wait_recv()
-    if STOP >= 3:
-        swap.wait_send()
-        for j in range(1, NC // 2):
-
-            @pl.when(j > chip)
-            def _():
-                state_copy(j).wait_send()
-
+    if STOP < 5:
+        if STOP < 4:
+            for copy in wcopies[3:]:
+                copy.wait()
+        settle()
     if STOP >= 5:
         for n in range(2):
-
-            @pl.when(core == 0)
-            def _():
-                kv_copy(kv.at[n], c, n, ks.at[0, n], sibling).wait_send()
-
-            for j in range(1, NC // 2):
-
-                @pl.when(kv_goes(j, n))
-                def _():
-                    kv_copy(kv.at[n], c, n, ks.at[j, n], 2 * j + core).wait_send()
-
             for j in range(half, 2 * half):
 
                 @pl.when(jnp.logical_and(chip >= half, j != chip) if TREE[n] else False)
@@ -650,6 +668,25 @@
                 return 0
 
             lax.fori_loop(0, chip, passed, 0)
+        att_copy.wait()
+
+
+def write(mixed_in, attended_in, mixed, attended, one, two, sem):
+    loads = (
+        pltpu.make_async_copy(mixed_in, one, sem.at[0]),
+        pltpu.make_async_copy(attended_in, two, sem.at[1]),
+    )
+    stores = (
+        pltpu.make_async_copy(one, mixed, sem.at[2]),
+        pltpu.make_async_copy(two, attended, sem.at[3]),
+    )
+    for copy in loads:
+        copy.start()
+    for load, store in zip(loads, stores):
+        load.wait()
+        store.start()
+    for copy in stores:
+        copy.wait()
 
 
 def local(residual, hyena_gain, in_weight, short_filter, decay_rate, residue, skip_gain, attn_gain, qkv_weight):
@@ -657,7 +694,7 @@
     vmem = pl.BlockSpec(memory_space=pltpu.VMEM)
     hbm = pl.BlockSpec(memory_space=pltpu.MemorySpace.HBM)
     dma = pltpu.SemaphoreType.DMA
-    return pl.pallas_call(
+    done = pl.pallas_call(
         kernel,
         out_shape=(
             jax.ShapeDtypeStruct((ROWS, WIDTH), bf16),
@@ -738,6 +775,22 @@
         far.reshape(NC, 1, -1),
         near,
     )
+    return pl.pallas_call(
+        write,
+        out_shape=(
+            jax.ShapeDtypeStruct((ROWS, WIDTH), bf16),
+            jax.ShapeDtypeStruct((ROWS, HD), bf16),
+        ),
+        in_specs=[hbm, hbm],
+        out_specs=(hbm, hbm),
+        scratch_shapes=[
+            pltpu.VMEM((ROWS, WIDTH), bf16),
+            pltpu.VMEM((ROWS, HD), bf16),
+            dma((4,)),
+        ],
+        compiler_params=pltpu.CompilerParams(vmem_limit_bytes=56 << 20),
+        name="write",
+    )(*done)
 
 
 def solution(mesh):

time: 79.5 us -> 77.3 us (0.972)
  local copies, waits for them, and re-layouts: 3.04 us -> 0 us
  Pallas kernels: 75.7 us -> 76.5 us
    unnamed x2 -> x0, local copies, waits for them, and re-layouts: 3.04 us -> none
    pallas_call x0 -> x1, Pallas kernels: none -> 1.61 us  [local(): pl.pallas_call(write, out_shape=(jax.ShapeDtypeStruct((ROWS, WIDTH), bf16...]
where the time goes in v3:
time: 77.3 us; the launch traced here: 77.2 us
  Pallas kernels  76.5 us (99%)
    pallas_call x1, Pallas kernels, local(): pl.pallas_call(kernel, out_shape=(jax.ShapeDtypeStruct((ROWS, WIDTH), bf1...  74.9 us
    pallas_call x1, Pallas kernels, local(): pl.pallas_call(write, out_shape=(jax.ShapeDtypeStruct((ROWS, WIDTH), bf16...  1.61 us

profile of v3, /device:TPU:3, one launch (start us, length us, event | category | flops | bytes accessed | tf_op | source)
XLA Modules:
  0.0 77.2 jit_solution(3563593253359460232)
XLA Ops:
  0.6 74.9 %genome.1 = (bf16[256,256]{1,0:T(8,128)(2,1)}, bf16[256,128]{1,0:T(8,128)(2,1)}) custom-call(bf16[256,256]{1,0:T(8,128)(2,1)} %res_h.1, f32[1,4096]{1,0:T(1,128)} %bitcast.9, bf16[3,4096,256]{2,1,0:T(8,128)(2,1)} %bitcast.7, f32[3,3,256]{2,1,0:T(4,128)} %taps_h.1, f32[16,256]{1,0:T(8,128)} %bitcast.10, f32[16,256]{1,0:T(8,128)} %bitcast.11, ...), custom_call_target="tpu_custom_call" | custom-call | tf_op jit(solution)/shard_map/genome/pallas_call | solution.py:697
  75.6 1.6 %write.1 = (bf16[256,256]{1,0:T(8,128)(2,1)}, bf16[256,128]{1,0:T(8,128)(2,1)}) custom-call(bf16[256,256]{1,0:T(8,128)(2,1)} %get-tuple-element.4.mixed_in, bf16[256,128]{1,0:T(8,128)(2,1)} %get-tuple-element.5.attended_in), custom_call_target="tpu_custom_call" | custom-call | tf_op jit(solution)/shard_map/write/pallas_call | solution.py:778

commit v4 on v3

--- a/solution.py
+++ b/solution.py
@@ -28,7 +28,7 @@
 DESC = 1
 UN = 4
 LAG0 = 8
-LAG1 = 3
+LAG1 = 6
 NOFOLD = 0
 DIST = 4
 PARTS1 = (((0, 80, 0), (80, 48, 1), (128, 80, 0), (208, 48, 1)),)
@@ -464,7 +464,7 @@
         lax.fori_loop(0, SPAN, spread, begin, unroll=UN)
         for k in range(2):
             cols = pl.ds(k * 128, 128)
-            g2[h, :, cols] = (g1[h, :, cols].astype(f32) + gate[k]).astype(bf16)
+            g2[h, :, cols] = (g1[h, :, cols].astype(f32) + gate[k, pl.ds(0, ROWS), :]).astype(bf16)
 
     if STOP >= 4:
         out_copy = pltpu.make_async_copy(g2.at[h], mixed, osem)
@@ -619,6 +619,12 @@
                 attend((kvs.at[org, n], kvs.at[other, n]), False)
 
         attend((kv.at[0], kv.at[1]), True)
+
+        def pass_first(k, _):
+            pass_on(k, 0)
+            return 0
+
+        lax.fori_loop(0, chip, pass_first, 0)
         relay(1)
 
         @pl.when(core == 1)
@@ -627,23 +633,25 @@
                 kv_copy(kv.at[n], c - 1, n, ks.at[0, n], 0).wait_recv()
             attend((kvs.at[c - 1, 0], kvs.at[c - 1, 1]), False)
 
-        for n in range(2):
-            if n == 1:
-                settle()
-            lag = (LAG0, LAG1)[n]
-
-            def lagged(k, _):
-                @pl.when(k < chip)
-                def _():
-                    pass_on(k, n)
-
-                @pl.when(k >= lag)
-                def _():
-                    both_cores(k - lag, n)
-
-                return 0
-
-            lax.fori_loop(0, jnp.where(chip > 0, chip + lag, 0), lagged, 0)
+        def attend_first(k, _):
+            both_cores(k, 0)
+            return 0
+
+        lax.fori_loop(0, chip, attend_first, 0)
+        settle()
+
+        def lagged(k, _):
+            @pl.when(k < chip)
+            def _():
+                pass_on(k, 1)
+
+            @pl.when(k >= LAG1)
+            def _():
+                both_cores(k - LAG1, 1)
+
+            return 0
+
+        lax.fori_loop(0, jnp.where(chip > 0, chip + LAG1, 0), lagged, 0)
 
         att[...] = (o_s[...] / l_s[...]).T.astype(bf16)
         att_copy = pltpu.make_async_copy(att, attended, asem)
@@ -718,7 +726,7 @@
             pltpu.VMEM((ROWS, 3 * WIDTH), f32),
             pltpu.VMEM((ROWS, 3 * HD), f32),
             pltpu.VMEM((ROWS, 128), f32),
-            pltpu.VMEM((6, ROWS + 8, 128), f32),
+            pltpu.VMEM((6, ROWS + 8 + SPAN, 128), f32),
             pltpu.VMEM((16, 3 * WIDTH), bf16),
             pltpu.VMEM((16, 3 * WIDTH), bf16),
             pltpu.VMEM((MODES, WIDTH), f32),
@@ -730,7 +738,7 @@
             pltpu.VMEM((SPAN, CHUNKS, WIDTH), f32),
             pltpu.VMEM((SPAN, CHUNKS, WIDTH), f32),
             pltpu.VMEM((MODES, CHUNKS, WIDTH), f32),
-            pltpu.VMEM((2, ROWS, 128), f32),
+            pltpu.VMEM((2, ROWS + SPAN, 128), f32),
             pltpu.VMEM((MODES, WIDTH), f32),
             pltpu.VMEM((NC // 2, MODES, WIDTH), f32),
             pltpu.VMEM((MODES, WIDTH), f32),

time: 77.3 us -> 76.9 us (level)
  no operation moved by 1% of the time
where the time goes in v4:
time: 76.9 us; the launch traced here: 76.8 us
  Pallas kernels  76.2 us (99%)
    pallas_call x1, Pallas kernels, local(): pl.pallas_call(kernel, out_shape=(jax.ShapeDtypeStruct((ROWS, WIDTH), bf1...  74.6 us
    pallas_call x1, Pallas kernels, local(): pl.pallas_call(write, out_shape=(jax.ShapeDtypeStruct((ROWS, WIDTH), bf16...  1.61 us

profile of v4, /device:TPU:3, one launch (start us, length us, event | category | flops | bytes accessed | tf_op | source)
XLA Modules:
  0.0 76.8 jit_solution(18110693053336707453)
XLA Ops:
  0.6 74.6 %genome.1 = (bf16[256,256]{1,0:T(8,128)(2,1)}, bf16[256,128]{1,0:T(8,128)(2,1)}) custom-call(bf16[256,256]{1,0:T(8,128)(2,1)} %res_h.1, f32[1,4096]{1,0:T(1,128)} %bitcast.9, bf16[3,4096,256]{2,1,0:T(8,128)(2,1)} %bitcast.7, f32[3,3,256]{2,1,0:T(4,128)} %taps_h.1, f32[16,256]{1,0:T(8,128)} %bitcast.10, f32[16,256]{1,0:T(8,128)} %bitcast.11, ...), custom_call_target="tpu_custom_call" | custom-call | tf_op jit(solution)/shard_map/genome/pallas_call | solution.py:705
  75.2 1.6 %write.1 = (bf16[256,256]{1,0:T(8,128)(2,1)}, bf16[256,128]{1,0:T(8,128)(2,1)}) custom-call(bf16[256,256]{1,0:T(8,128)(2,1)} %get-tuple-element.4.mixed_in, bf16[256,128]{1,0:T(8,128)(2,1)} %get-tuple-element.5.attended_in), custom_call_target="tpu_custom_call" | custom-call | tf_op jit(solution)/shard_map/write/pallas_call | solution.py:786

commit v5 on v4

--- a/solution.py
+++ b/solution.py
@@ -31,7 +31,7 @@
 LAG1 = 6
 NOFOLD = 0
 DIST = 4
-PARTS1 = (((0, 80, 0), (80, 48, 1), (128, 80, 0), (208, 48, 1)),)
+PARTS1 = (((0, 64, 0), (64, 32, 1), (96, 64, 0), (160, 32, 1), (192, 32, 0), (224, 32, 1)),)
 PARTS2 = (((0, 80, 0), (80, 48, 1)), ((128, 80, 0), (208, 48, 1)))
 GROUP = 128
 KVORDER = 1

time: 76.9 us -> 77.5 us (level)
  no operation moved by 1% of the time
where the time goes in v5:
time: 77.5 us; the launch traced here: 77.4 us
  Pallas kernels  76.7 us (99%)
    pallas_call x1, Pallas kernels, local(): pl.pallas_call(kernel, out_shape=(jax.ShapeDtypeStruct((ROWS, WIDTH), bf1...  75.1 us
    pallas_call x1, Pallas kernels, local(): pl.pallas_call(write, out_shape=(jax.ShapeDtypeStruct((ROWS, WIDTH), bf16...  1.61 us

profile of v5, /device:TPU:3, one launch (start us, length us, event | category | flops | bytes accessed | tf_op | source)
XLA Modules:
  0.0 77.4 jit_solution(6822125681277296278)
XLA Ops:
  0.6 75.1 %genome.1 = (bf16[256,256]{1,0:T(8,128)(2,1)}, bf16[256,128]{1,0:T(8,128)(2,1)}) custom-call(bf16[256,256]{1,0:T(8,128)(2,1)} %res_h.1, f32[1,4096]{1,0:T(1,128)} %bitcast.9, bf16[3,4096,256]{2,1,0:T(8,128)(2,1)} %bitcast.7, f32[3,3,256]{2,1,0:T(4,128)} %taps_h.1, f32[16,256]{1,0:T(8,128)} %bitcast.10, f32[16,256]{1,0:T(8,128)} %bitcast.11, ...), custom_call_target="tpu_custom_call" | custom-call | tf_op jit(solution)/shard_map/genome/pallas_call | solution.py:705
  75.8 1.6 %write.1 = (bf16[256,256]{1,0:T(8,128)(2,1)}, bf16[256,128]{1,0:T(8,128)(2,1)}) custom-call(bf16[256,256]{1,0:T(8,128)(2,1)} %get-tuple-element.4.mixed_in, bf16[256,128]{1,0:T(8,128)(2,1)} %get-tuple-element.5.attended_in), custom_call_target="tpu_custom_call" | custom-call | tf_op jit(solution)/shard_map/write/pallas_call | solution.py:786
